TPU v7x, 32 devices: a whole 2x2x4 slice. The times are simulated.
32 devices in a mesh: dpo: 4 (over z), dpi: 2 (over x), tp: 4 (over y, core).
Axes of the slice: x: 2, y: 2, z: 4, core: 2. Of those that a mesh axis runs over, the one named last changes fastest.
Arguments:
- tokens: bfloat16 [8192, 768], P(('dpo', 'dpi')), may hold values from -6 to 6
- cotangent: bfloat16 [8192, 768], P(('dpo', 'dpi')), may hold values from -6 to 6
- heights: int32 [32], P(('dpo', 'dpi')), may hold values from 1 to 15
- labels: int32 [32], P(('dpo', 'dpi')), may hold values from 0 to 999
- valid: int32 [8192], P(('dpo', 'dpi')), may hold values 0 or 1
- class_table: bfloat16 [1000, 768], replicated, may hold values from -6 to 6
- gains: float32 [2, 2, 768], replicated, may hold values from 0.25 to 1.75
- w_qkv: bfloat16 [2, 768, 3, 768], P(None, None, None, 'tp'), may hold values from -0.21875 to 0.21875
- w_out: bfloat16 [2, 768, 768], P(None, 'tp'), may hold values from -1.75 to 1.75
- w_gate_up: bfloat16 [2, 768, 2, 2048], P(None, None, None, 'tp'), may hold values from -0.21875 to 0.21875
- w_down: bfloat16 [2, 2048, 768], P(None, 'tp'), may hold values from -0.125 to 0.125
Outputs:
- output: float32 [8192, 768], P(('dpo', 'dpi'))
- token_grad: float32 [8192, 768], P(('dpo', 'dpi'))
- table_grad: float32 [1000, 768], P(None, 'dpi')
- gain_grad: float32 [2, 2, 768], replicated
- qkv_grad: float32 [2, 768, 3, 768], P(None, 'dpi', None, 'tp')
- out_grad: float32 [2, 768, 768], P(None, 'tp', 'dpi')
- gate_up_grad: float32 [2, 768, 2, 2048], P(None, 'dpi', None, 'tp')
- down_grad: float32 [2, 2048, 768], P(None, 'tp', 'dpi')
All inputs are finite; a program needn't handle non-finite values. No bound on the sum of `valid` on one device may be relied on, other than what follows from the above.
Results may differ from a plain program's by a relative error of at most 0.018.
Values sent between devices are 32-bit elements; how exact they have to be, the bound alone decides.
A program may use at most 128 MiB of HBM per device.

v0:
```python
import jax
import jax.numpy as jnp
from jax import lax
from jax.sharding import PartitionSpec as P

HD = 64
COLS = 16


epsilon = 1e-05


def rope_tables(slot_len):
    quarter = HD // 4
    position = jnp.arange(slot_len)
    raster = jnp.maximum(position - 1, 0)
    row_pos = (raster // COLS).astype(jnp.float32)
    col_pos = (raster % COLS).astype(jnp.float32)
    frequency = 10000.0 ** (-jnp.arange(quarter).astype(jnp.float32) / quarter)
    row_angle = (row_pos[:, None] * frequency[None, :])[:, None, :]
    col_angle = (col_pos[:, None] * frequency[None, :])[:, None, :]
    return (jnp.cos(row_angle), jnp.sin(row_angle), jnp.cos(col_angle), jnp.sin(col_angle))


def rotate_pairs(values_in, tables, direction):
    quarter = values_in.shape[-1] // 4
    cos_row, sin_row, cos_col, sin_col = tables
    sin_row = sin_row * direction
    sin_col = sin_col * direction
    first_part = values_in[..., :quarter]
    second_part = values_in[..., quarter : 2 * quarter]
    third_part = values_in[..., 2 * quarter : 3 * quarter]
    fourth_part = values_in[..., 3 * quarter :]
    return jnp.concatenate(
        [
            first_part * cos_row - second_part * sin_row,
            second_part * cos_row + first_part * sin_row,
            third_part * cos_col - fourth_part * sin_col,
            fourth_part * cos_col + third_part * sin_col,
        ],
        axis=-1,
    )


def visible(heights, valid, slot_len):
    position = jnp.arange(slot_len)
    length = 1 + COLS * heights
    open_key = (position[None, :] < length[:, None]) & (valid == 1)
    causal = position[:, None] >= position[None, :]
    diagonal = position[:, None] == position[None, :]
    return causal[None] & (open_key[:, None, :] | diagonal[None])


def score_block(queries, key_rows, allowed):
    scores = jnp.einsum(
        "sihd,sjhd->shij", queries, key_rows, preferred_element_type=jnp.float32
    ) * HD ** (-0.5)
    return jnp.where(allowed[:, None], scores, -jnp.inf)


def norm_back(grad_out, normed, scale_inv, gain):
    scaled = grad_out * gain
    return scale_inv * (scaled - normed * jnp.mean(scaled * normed, axis=-1, keepdims=True))


def on_device(
    tokens, cotangent, heights, labels, valid, class_table, gains, w_qkv, w_out, w_gate_up, w_down
):
    seq_count = heights.shape[0]
    row_count = tokens.shape[0]
    slot_len = row_count // seq_count
    model_width = tokens.shape[1]
    layers = gains.shape[0]
    local_heads = w_out.shape[1] // HD
    allowed = visible(heights, valid.reshape(seq_count, slot_len), slot_len)
    tables = rope_tables(slot_len)
    onehot = labels[:, None] == jnp.arange(class_table.shape[0])[None, :]
    first_rows = jnp.dot(
        onehot.astype(jnp.bfloat16), class_table, preferred_element_type=jnp.float32
    )
    token_grid = tokens.astype(jnp.float32).reshape(seq_count, slot_len, model_width)
    residual = jnp.concatenate([first_rows[:, None], token_grid[:, 1:]], axis=1).reshape(
        row_count, model_width
    )
    kept_layers = []
    for layer_index in range(layers):
        scale_one = lax.rsqrt(jnp.mean(residual * residual, axis=-1, keepdims=True) + epsilon)
        normed_one = residual * scale_one
        attn_in = (normed_one * gains[layer_index, 0]).astype(jnp.bfloat16)
        packed = jnp.einsum(
            "nd,dta->nta", attn_in, w_qkv[layer_index], preferred_element_type=jnp.float32
        )
        shaped = packed.reshape(seq_count, slot_len, 3, local_heads, HD)
        queries = rotate_pairs(shaped[:, :, 0], tables, 1.0).astype(jnp.bfloat16)
        key_rows = rotate_pairs(shaped[:, :, 1], tables, 1.0).astype(jnp.bfloat16)
        value_rows = shaped[:, :, 2].astype(jnp.bfloat16)
        scores = score_block(queries, key_rows, allowed)
        largest = jnp.max(scores, axis=-1, keepdims=True)
        raised = jnp.exp(scores - largest)
        row_total = jnp.sum(raised, axis=-1, keepdims=True)
        attn_prob = (raised / row_total).astype(jnp.bfloat16)
        log_total = largest + jnp.log(row_total)
        mixed_heads = jnp.einsum(
            "shij,sjhd->sihd", attn_prob, value_rows, preferred_element_type=jnp.float32
        )
        mixed_heads = mixed_heads.astype(jnp.bfloat16).reshape(row_count, local_heads * HD)
        branch = lax.psum(
            jnp.dot(mixed_heads, w_out[layer_index], preferred_element_type=jnp.float32), "tp"
        )
        middle = residual + branch
        scale_two = lax.rsqrt(jnp.mean(middle * middle, axis=-1, keepdims=True) + epsilon)
        normed_two = middle * scale_two
        mlp_in = (normed_two * gains[layer_index, 1]).astype(jnp.bfloat16)
        pair_value = jnp.einsum(
            "nd,dtf->ntf", mlp_in, w_gate_up[layer_index], preferred_element_type=jnp.float32
        )
        gate_value = pair_value[:, 0]
        up_value = pair_value[:, 1]
        hidden = (jax.nn.silu(gate_value) * up_value).astype(jnp.bfloat16)
        kept_layers.append(
            (
                scale_one,
                normed_one,
                attn_in,
                queries,
                key_rows,
                value_rows,
                log_total,
                mixed_heads,
                scale_two,
                normed_two,
                mlp_in,
                gate_value,
                up_value,
                hidden,
            )
        )
        residual = middle + lax.psum(
            jnp.dot(hidden, w_down[layer_index], preferred_element_type=jnp.float32), "tp"
        )
    grad_state = cotangent.astype(jnp.float32)
    qkv_list, out_list, gate_up_list, down_list, gain_list = ([], [], [], [], [])
    for layer_index in reversed(range(layers)):
        (
            scale_one,
            normed_one,
            attn_in,
            queries,
            key_rows,
            value_rows,
            log_total,
            mixed_heads,
            scale_two,
            normed_two,
            mlp_in,
            gate_value,
            up_value,
            hidden,
        ) = kept_layers[layer_index]
        mlp_grad = grad_state.astype(jnp.bfloat16)
        down_list.append(
            jnp.einsum("nf,nd->fd", hidden, mlp_grad, preferred_element_type=jnp.float32)
        )
        hidden_grad = jnp.einsum(
            "nd,fd->nf", mlp_grad, w_down[layer_index], preferred_element_type=jnp.float32
        )
        sigmoid_gate = jax.nn.sigmoid(gate_value)
        silu_value = gate_value * sigmoid_gate
        silu_slope = sigmoid_gate * (1.0 + gate_value * (1.0 - sigmoid_gate))
        pair_grad = jnp.stack(
            [hidden_grad * up_value * silu_slope, hidden_grad * silu_value], axis=1
        ).astype(jnp.bfloat16)
        gate_up_list.append(
            jnp.einsum("nd,ntf->dtf", mlp_in, pair_grad, preferred_element_type=jnp.float32)
        )
        norm_part = jnp.einsum(
            "ntf,dtf->nd", pair_grad, w_gate_up[layer_index], preferred_element_type=jnp.float32
        )
        gain_two = jnp.sum(norm_part * normed_two, axis=0)
        norm_full = lax.psum(norm_part, "tp")
        grad_mid = grad_state + norm_back(norm_full, normed_two, scale_two, gains[layer_index, 1])
        attn_grad = grad_mid.astype(jnp.bfloat16)
        out_list.append(
            jnp.einsum("na,nd->ad", mixed_heads, attn_grad, preferred_element_type=jnp.float32)
        )
        mixed_grad = jnp.einsum(
            "nd,ad->na", attn_grad, w_out[layer_index], preferred_element_type=jnp.float32
        )
        mixed_grad = mixed_grad.astype(jnp.bfloat16).reshape(seq_count, slot_len, local_heads, HD)
        scores = score_block(queries, key_rows, allowed)
        attn_prob = jnp.exp(scores - log_total)
        prob_grad = jnp.einsum(
            "sihd,sjhd->shij", mixed_grad, value_rows, preferred_element_type=jnp.float32
        )
        score_grad = (
            attn_prob * (prob_grad - jnp.sum(attn_prob * prob_grad, axis=-1, keepdims=True))
        ).astype(jnp.bfloat16)
        value_grad = jnp.einsum(
            "shij,sihd->sjhd",
            attn_prob.astype(jnp.bfloat16),
            mixed_grad,
            preferred_element_type=jnp.float32,
        ).astype(jnp.bfloat16)
        query_grad = jnp.einsum(
            "shij,sjhd->sihd", score_grad, key_rows, preferred_element_type=jnp.float32
        ) * HD ** (-0.5)
        query_grad = rotate_pairs(query_grad, tables, -1.0).astype(jnp.bfloat16)
        key_grad = jnp.einsum(
            "shij,sihd->sjhd", score_grad, queries, preferred_element_type=jnp.float32
        ) * HD ** (-0.5)
        key_grad = rotate_pairs(key_grad, tables, -1.0).astype(jnp.bfloat16)
        packed_grad = jnp.stack([query_grad, key_grad, value_grad], axis=2).reshape(
            row_count, 3, local_heads * HD
        )
        qkv_list.append(
            jnp.einsum("nd,nta->dta", attn_in, packed_grad, preferred_element_type=jnp.float32)
        )
        norm_part = jnp.einsum(
            "nta,dta->nd", packed_grad, w_qkv[layer_index], preferred_element_type=jnp.float32
        )
        gain_one = jnp.sum(norm_part * normed_one, axis=0)
        norm_full = lax.psum(norm_part, "tp")
        grad_state = grad_mid + norm_back(norm_full, normed_one, scale_one, gains[layer_index, 0])
        gain_list.append(jnp.stack([gain_one, gain_two], axis=0))
    grid_grad = grad_state.reshape(seq_count, slot_len, model_width)
    position = jnp.arange(slot_len)
    token_grad = jnp.where((position == 0)[None, :, None], 0.0, grid_grad).reshape(
        row_count, model_width
    )
    table_grad = jnp.einsum(
        "sc,sd->cd", onehot.astype(jnp.float32), grid_grad[:, 0], precision=lax.Precision.HIGHEST
    )
    qkv_all = jnp.stack(qkv_list[::-1], axis=0)
    out_all = jnp.stack(out_list[::-1], axis=0)
    gate_up_all = jnp.stack(gate_up_list[::-1], axis=0)
    down_all = jnp.stack(down_list[::-1], axis=0)
    gain_all = jnp.stack(gain_list[::-1], axis=0)
    shards = (
        lax.psum_scatter(qkv_all, "dpi", scatter_dimension=1, tiled=True),
        lax.psum_scatter(out_all, "dpi", scatter_dimension=2, tiled=True),
        lax.psum_scatter(gate_up_all, "dpi", scatter_dimension=1, tiled=True),
        lax.psum_scatter(down_all, "dpi", scatter_dimension=2, tiled=True),
        lax.psum_scatter(table_grad, "dpi", scatter_dimension=1, tiled=True),
    )
    qkv_part, out_part, gate_up_part, down_part, table_part = lax.psum(
        (shards[0], shards[1], shards[2], shards[3], shards[4]), "dpo"
    )
    gain_total = lax.psum(gain_all, ("dpo", "dpi", "tp"))
    return (
        residual,
        token_grad,
        table_part,
        gain_total,
        qkv_part,
        out_part,
        gate_up_part,
        down_part,
    )


def solution(mesh):
    placed = (
        P(("dpo", "dpi"), None),
        P(("dpo", "dpi"), None),
        P(("dpo", "dpi")),
        P(("dpo", "dpi")),
        P(("dpo", "dpi")),
        P(),
        P(),
        P(None, None, None, "tp"),
        P(None, "tp", None),
        P(None, None, None, "tp"),
        P(None, "tp", None),
    )
    return jax.shard_map(
        on_device,
        mesh=mesh,
        in_specs=placed,
        out_specs=(
            P(("dpo", "dpi"), None),
            P(("dpo", "dpi"), None),
            P(None, "dpi"),
            P(),
            P(None, "dpi", None, "tp"),
            P(None, "tp", "dpi"),
            P(None, "dpi", None, "tp"),
            P(None, "tp", "dpi"),
        ),
        check_vma=False,
    )
```

profile of v0, /device:TPU:0, one launch (start us, length us, event | category | flops | bytes accessed | tf_op | source)
XLA Modules:
  0.0 1259.4 jit_solution(6122839863150992163)
XLA Ops:
  28.3 5.2 fusion.154
  33.5 66.0 %all-reduce.11.cloned.1.call-done = f32[1024,768]{1,0:T(8,128)} async-done(((f32[1024,768]{1,0:T(8,128)}), f32[1024,768]{1,0:T(8,128)}) %all-reduce.11.cloned.1.call-update) | async-done | bytes 3145744 | tf_op jit(solution)/shard_map/psum | solution.py:107
  109.2 68.4 %all-reduce.13.cloned.1.call-done = f32[1024,768]{1,0:T(8,128)} async-done(((f32[1024,768]{1,0:T(8,128)}), f32[1024,768]{1,0:T(8,128)}) %all-reduce.13.cloned.1.call-update) | async-done | bytes 3145744 | tf_op jit(solution)/shard_map/psum | solution.py:138
  177.6 3.3 multiply_reduce_fusion.11
  190.9 68.6 %all-reduce.15.cloned.1.call-done = f32[1024,768]{1,0:T(8,128)} async-done(((f32[1024,768]{1,0:T(8,128)}), f32[1024,768]{1,0:T(8,128)}) %all-reduce.15.cloned.1.call-update) | async-done | bytes 3145744 | tf_op jit(solution)/shard_map/psum | solution.py:107
  259.6 3.4 multiply_reduce_fusion.10
  269.4 3.5 convolution_bitcast_fusion.5
  274.0 67.6 %all-reduce.17.cloned.1.call-done = f32[1024,768]{1,0:T(8,128)} async-done(((f32[1024,768]{1,0:T(8,128)}), f32[1024,768]{1,0:T(8,128)}) %all-reduce.17.cloned.1.call-update) | async-done | bytes 3145744 | tf_op jit(solution)/shard_map/psum | solution.py:180
  341.6 5.3 multiply_reduce_fusion
  375.7 4.3 convolution_bitcast_fusion.4
  380.1 68.6 %all-reduce.19.cloned.1.call-done = f32[1024,768]{1,0:T(8,128)} async-done(((f32[1024,768]{1,0:T(8,128)}), f32[1024,768]{1,0:T(8,128)}) %all-reduce.19.cloned.1.call-update) | async-done | bytes 3145744 | tf_op jit(solution)/shard_map/psum | solution.py:222
  448.8 5.3 multiply_reduce_fusion.1
  461.1 3.6 convolution_bitcast_fusion.3
  466.0 5.3 fusion.61
  471.3 62.1 %all-reduce.21.cloned.1.call-done = f32[1024,768]{1,0:T(8,128)} async-done(((f32[1024,768]{1,0:T(8,128)}), f32[1024,768]{1,0:T(8,128)}) %all-reduce.21.cloned.1.call-update) | async-done | bytes 3145744 | tf_op jit(solution)/shard_map/psum | solution.py:180
  533.4 5.3 multiply_reduce_fusion.2
  568.0 4.3 convolution_bitcast_fusion.2
  577.3 4.9 convolution_bitcast_fusion.6
  587.0 105.4 %all-reduce.23.cloned.1.call-done = (f32[1024,768]{1,0:T(8,128)}, f32[1024,768]{1,0:T(8,128)}) async-done(((f32[1024,768]{1,0:T(8,128)}, f32[1024,768]{1,0:T(8,128)}), (f32[1024,768]{1,0:T(8,128)}, f32[1024,768]{1,0:T(8,128)})) %all-reduce.23.cloned.1.call-update) | async-done | bytes 6291472 | tf_op jit(solution)/shard_map/psum | solution.py:138
  692.4 3.9 multiply_reduce_fusion.3
  697.0 3.0 broadcast_select_fusion
  700.1 3.2 fusion.127
  710.0 4.8 convolution_bitcast_fusion
  716.7 3.3 pad_maximum_fusion
  720.2 42.1 %reduce-scatter.14.cloned.1.call-done = f32[2,512,384]{2,1,0:T(8,128)} async-done(((f32[2,512,768]{2,1,0:T(8,128)}), f32[2,512,384]{2,1,0:T(8,128)}) %reduce-scatter.14.cloned.1.call-update) | async-done | bytes 1572880 | tf_op jit(solution)/shard_map/reduce_scatter | solution.py:242
  762.3 44.7 %reduce-scatter.6.cloned.1.call-done = f32[1000,384]{1,0:T(8,128)} async-done(((f32[1000,768]{1,0:T(8,128)}), f32[1000,384]{1,0:T(8,128)}) %reduce-scatter.6.cloned.1.call-update) | async-done | bytes 1536016 | tf_op jit(solution)/shard_map/reduce_scatter | solution.py:243
  807.0 50.0 %reduce-scatter.8.cloned.1.call-done = f32[2,384,3,192]{1,3,2,0:T(8,128)} async-done(((f32[2,768,3,192]{1,3,2,0:T(8,128)}), f32[2,384,3,192]{1,3,2,0:T(8,128)}) %reduce-scatter.8.cloned.1.call-update) | async-done | bytes 1769488 | tf_op jit(solution)/shard_map/reduce_scatter | solution.py:239
  857.0 79.3 %reduce-scatter.12.cloned.1.call-done = f32[2,384,2,512]{3,1,2,0:T(8,128)} async-done(((f32[2,768,2,512]{3,1,2,0:T(8,128)}), f32[2,384,2,512]{3,1,2,0:T(8,128)}) %reduce-scatter.12.cloned.1.call-update) | async-done | bytes 3145744 | tf_op jit(solution)/shard_map/reduce_scatter | solution.py:241
  938.2 3.9 add.288
  942.2 43.3 %psum.107 = f32[2,2,768]{2,1,0:T(2,128)} all-reduce(f32[2,2,768]{2,1,0:T(2,128)S(1)} %pad_maximum_fusion.27), channel_id=1, replica_groups=mesh['dpo'=4,'dpi'=2,'tp'=4] {'dpo','dpi','tp'}, use_global_device_ids=true, to_apply=%region_28.29 | all-reduce | flops 3072 | bytes 24576 | tf_op jit(solution)/shard_map/psum | solution.py:248
  985.5 256.5 %all-reduce.25.cloned.1.call-done = (f32[1000,384]{1,0:T(8,128)}, f32[2,384,3,192]{1,3,2,0:T(8,128)}, f32[2,192,384]{2,1,0:T(8,128)}, f32[2,384,2,512]{3,1,2,0:T(8,128)}, f32[2,512,384]{2,1,0:T(8,128)}) async-done(((f32[1000,384]{1,0:T(8,128)}, f32[2,384,3,192]{1,3,2,0:T(8,128)}, f32[2,192,384]{2,1,0:T(8,128)}, f32[2,384,2,512]{3,1,2,0:T(8,128)}, f32[2,512,384]{2,1,0:T(8,128)}), (f32[1000,384]{1,0:T(8,128)}, ...) | async-done | bytes 8613904 | tf_op jit(solution)/shard_map/psum | solution.py:245
  1242.0 6.1 copy.68
  (397 shorter events, 138.9 us)
Async XLA Ops:
  7.2 92.4 %all-reduce.11.cloned.1.call-start = ((), (), s32[]{:S(2)}) async-start(), calls=%async_computation.5 | async-start | bytes 6291456 | tf_op jit(solution)/shard_map/psum | solution.py:107
  8.8 93.3 %copy-start.94 = (f32[768]{0:T(1024)}, f32[768]{0:T(1024)S(1)}, u32[]{:S(2)}) copy-start(f32[768]{0:T(1024)S(1)} %get-tuple-element.33) | copy-start | bytes 9220
  8.8 172.1 %copy-start.86 = (f32[768]{0:T(1024)}, f32[768]{0:T(1024)S(1)}, u32[]{:S(2)}) copy-start(f32[768]{0:T(1024)S(1)} %get-tuple-element.35) | copy-start | bytes 9220
  8.8 338.1 %copy-start.100 = (f32[768]{0:T(1024)}, f32[768]{0:T(1024)S(1)}, u32[]{:S(2)}) copy-start(f32[768]{0:T(1024)S(1)} %get-tuple-element.32) | copy-start | bytes 9220
  17.1 167.2 %copy-start.46 = (f32[256,16]{0,1:T(8,128)}, f32[256,16]{0,1:T(8,128)S(1)}, u32[]{:S(2)}) copy-start(f32[256,16]{0,1:T(8,128)S(1)} %get-tuple-element.123) | copy-start | bytes 49156
  28.3 149.3 %all-reduce.13.cloned.1.call-start = ((), (), s32[]{:S(2)}) async-start(), calls=%async_computation.6 | async-start | bytes 6291456 | tf_op jit(solution)/shard_map/psum | solution.py:138
  108.9 150.7 %all-reduce.15.cloned.1.call-start = ((), (), s32[]{:S(2)}) async-start(), calls=%async_computation.7 | async-start | bytes 6291456 | tf_op jit(solution)/shard_map/psum | solution.py:107
  190.9 150.7 %all-reduce.17.cloned.1.call-start = ((), (), s32[]{:S(2)}) async-start(), calls=%async_computation.8 | async-start | bytes 6291456 | tf_op jit(solution)/shard_map/psum | solution.py:180
  263.0 83.9 %copy-start.102 = (f32[1024]{0:T(1024)}, f32[1024]{0:T(1024)S(1)}, u32[]{:S(2)}) copy-start(f32[1024]{0:T(1024)S(1)} %add_rsqrt_fusion) | copy-start | bytes 12292
  272.9 175.8 %all-reduce.19.cloned.1.call-start = ((), (), s32[]{:S(2)}) async-start(), calls=%async_computation.9 | async-start | bytes 6291456 | tf_op jit(solution)/shard_map/psum | solution.py:222
  341.6 5.6 copy-start.24
  341.6 6.0 copy-start.44
  380.0 68.7 %copy-start.87 = (f32[768]{0:T(1024)S(1)}, f32[768]{0:T(1024)}, u32[]{:S(2)}) copy-start(f32[768]{0:T(1024)} %copy-done.86) | copy-start | bytes 9220
  380.0 68.7 %copy-start.89 = (f32[1024]{0:T(1024)S(1)}, f32[1024]{0:T(1024)}, u32[]{:S(2)}) copy-start(f32[1024]{0:T(1024)} %copy-done.88) | copy-start | bytes 12292
  380.1 153.3 %all-reduce.21.cloned.1.call-start = ((), (), s32[]{:S(2)}) async-start(), calls=%async_computation.10 | async-start | bytes 6291456 | tf_op jit(solution)/shard_map/psum | solution.py:180
  448.8 5.6 copy-start.18
  448.8 6.5 copy-start.25
  464.7 227.7 %all-reduce.23.cloned.1.call-start = ((), (), s32[]{:S(2)}) async-start(), calls=%async_computation.16 | async-start | bytes 12582912 | tf_op jit(solution)/shard_map/psum | solution.py:138
  466.0 67.4 %copy-start.95 = (f32[768]{0:T(1024)S(1)}, f32[768]{0:T(1024)}, u32[]{:S(2)}) copy-start(f32[768]{0:T(1024)} %copy-done.94) | copy-start | bytes 9220
  466.0 67.4 %copy-start.98 = (f32[1024]{0:T(1024)S(1)}, f32[1024]{0:T(1024)}, u32[]{:S(2)}) copy-start(f32[1024]{0:T(1024)} %copy-done.97) | copy-start | bytes 12292
  533.4 5.6 copy-start.21
  533.4 6.5 copy-start.23
  572.3 147.9 %reduce-scatter.10.cloned.1.call-start = ((), (), s32[]{:S(2)}) async-start(), calls=%async_computation.13 | async-start | bytes 1769472 | tf_op jit(solution)/shard_map/reduce_scatter | solution.py:240
  577.0 185.3 %reduce-scatter.14.cloned.1.call-start = ((), (), s32[]{:S(2)}) async-start(), calls=%async_computation.15 | async-start | bytes 4718592 | tf_op jit(solution)/shard_map/reduce_scatter | solution.py:242
  577.3 5.7 copy-start.117
  586.2 106.1 %copy-start.81 = (f32[768]{0:T(1024)S(1)}, f32[768]{0:T(1024)}, u32[]{:S(2)}) copy-start(f32[768]{0:T(1024)} %copy-done.80) | copy-start | bytes 9220
  586.3 220.7 %reduce-scatter.6.cloned.1.call-start = ((), (), s32[]{:S(2)}) async-start(), calls=%async_computation.11 | async-start | bytes 4608000 | tf_op jit(solution)/shard_map/reduce_scatter | solution.py:243
  703.3 153.7 %reduce-scatter.8.cloned.1.call-start = ((), (), s32[]{:S(2)}) async-start(), calls=%async_computation.12 | async-start | bytes 5308416 | tf_op jit(solution)/shard_map/reduce_scatter | solution.py:239
  709.3 226.9 %reduce-scatter.12.cloned.1.call-start = ((), (), s32[]{:S(2)}) async-start(), calls=%async_computation.14 | async-start | bytes 9437184 | tf_op jit(solution)/shard_map/reduce_scatter | solution.py:241
  720.1 521.9 %all-reduce.25.cloned.1.call-start = ((), (), s32[]{:S(2)}) async-start(), calls=%async_computation.17 | async-start | bytes 17227776 | tf_op jit(solution)/shard_map/psum | solution.py:245
  1242.0 6.1 copy-start.45
  1242.0 7.3 copy-start.36
  (106 other events, 255.1 us)
Sparse Core Ops, SparseCore 0:
  28.4 71.1 all-reduce.10
  109.0 68.5 all-reduce.12
  191.0 68.5 all-reduce.14
  273.1 68.5 all-reduce.16
  380.2 68.5 all-reduce.18
  464.8 68.5 all-reduce.20
  572.4 119.8 all-reduce.22
  694.6 21.9 reduce-scatter.9
  718.9 43.3 reduce-scatter.13
  764.4 42.5 reduce-scatter.5
  809.3 47.6 reduce-scatter.7
  859.2 77.0 reduce-scatter.11
  939.7 302.2 all-reduce.24
where the time goes:
time: 1270 us; the launch traced here: 1260 us
  waiting for transfers between devices  980 us (77%)
  matrix products  84.6 us (7%)
  local copies, waits for them, and re-layouts  70.8 us (6%)
  other arithmetic  63.3 us (5%)
  blocking collectives  43.3 us (3%)
  between operations  15.9 us (1%)
    psum x1, waiting for transfers between devices, on_device(): lax.psum((shards[0], shards[1], shards[2], shards[3], shards[4]), 'dpo')  257 us
    psum x3, waiting for transfers between devices, on_device(): norm_full = lax.psum(norm_part, 'tp')  198 us
    psum x2, waiting for transfers between devices, on_device(): lax.psum(jnp.dot(hidden, w_down[layer_index], preferred_element_type=jnp....  174 us
    psum x2, waiting for transfers between devices, on_device(): lax.psum(jnp.dot(mixed_heads, w_out[layer_index], preferred_element_type=...  135 us
    reduce_scatter x1, waiting for transfers between devices, on_device(): lax.psum_scatter(gate_up_all, 'dpi', scatter_dimension=1, tiled=True)  79.3 us
    reduce_scatter x1, waiting for transfers between devices, on_device(): lax.psum_scatter(qkv_all, 'dpi', scatter_dimension=1, tiled=True)  50 us
    reduce_scatter x1, waiting for transfers between devices, on_device(): lax.psum_scatter(table_grad, 'dpi', scatter_dimension=1, tiled=True)  44.7 us
    unnamed x262, local copies, waits for them, and re-layouts  43.4 us
  transfers between devices with their start and end apart: 13, of which 12 were waited for; matrix products, arithmetic and copies ran while one was open for 4% of the time, Pallas kernels for 0%

commit v1 on v0

v1 whole, which is shorter than its diff:
```python
import functools

import jax
import jax.numpy as jnp
import numpy as np
from jax import lax
from jax.experimental import pallas as pl
from jax.experimental.pallas import tpu as pltpu
from jax.sharding import PartitionSpec as P

HD = 64
COLS = 16
EPS = 1e-05
F32 = jnp.float32
BF16 = jnp.bfloat16
LOW = -1e30

NN = (((1,), (0,)), ((), ()))
NT = (((1,), (1,)), ((), ()))
TN = (((0,), (0,)), ((), ()))


def mm(a, b, dims=NN):
    return lax.dot_general(a, b, dims, preferred_element_type=F32)


def rope_constants(slot_len):
    quarter = HD // 4
    raster = np.maximum(np.arange(slot_len) - 1, 0)
    row_pos = (raster // COLS).astype(np.float32)
    col_pos = (raster % COLS).astype(np.float32)
    frequency = (10000.0 ** (-np.arange(quarter).astype(np.float32) / quarter)).astype(np.float32)
    row_angle = row_pos[:, None] * frequency[None, :]
    col_angle = col_pos[:, None] * frequency[None, :]
    zero = np.zeros_like(row_angle)
    cos = np.concatenate([np.cos(row_angle)] * 2 + [np.cos(col_angle)] * 2, axis=1)
    first = np.concatenate([-np.sin(row_angle), zero, -np.sin(col_angle), zero], axis=1)
    second = np.concatenate([zero, np.sin(row_angle), zero, np.sin(col_angle)], axis=1)
    return np.stack([np.tile(t, (1, 2)) for t in (cos, first, second)]).astype(np.float32)


def rotate(x, table_ref, sign):
    quarter = HD // 4
    ahead = pltpu.roll(x, 2 * HD - quarter, 1) * table_ref[1]
    behind = pltpu.roll(x, quarter, 1) * table_ref[2]
    turned = ahead + behind
    return x * table_ref[0] + (turned if sign > 0 else -turned)


def merge(axis, mine_ref, other_ref, out_ref):
    size = mine_ref.shape[axis]
    if axis == 1:
        out_ref[:, :size, :] = mine_ref[...].astype(BF16)
        out_ref[:, size:, :] = other_ref[...].astype(BF16)
    else:
        out_ref[:, :, :size] = mine_ref[...].astype(BF16)
        out_ref[:, :, size:] = other_ref[...].astype(BF16)


def inv_rms(h):
    return lax.rsqrt(jnp.mean(h * h, axis=-1, keepdims=True) + EPS)


def norm_back(grad, normed, scale, gain):
    scaled = grad * gain
    return scale * (scaled - normed * jnp.mean(scaled * normed, axis=-1, keepdims=True))


def key_mask(open_ref, n):
    key = lax.broadcasted_iota(jnp.int32, (n, n), 0)
    query = lax.broadcasted_iota(jnp.int32, (n, n), 1)
    return ((key < query) & (open_ref[...] > 0.5)) | (key == query)


def attn_fwd(first, *refs):
    if first:
        h_ref, gain_ref, wqkv_ref, wout_ref, table_ref, open_ref = refs[:6]
        refs = refs[6:]
        h = h_ref[...]
    else:
        h_ref, p_ref, r_ref, gain_ref, wqkv_ref, wout_ref, table_ref, open_ref = refs[:8]
        refs = refs[8:]
        h = h_ref[...] + (p_ref[...] + r_ref[...])
        refs[0][...] = h
        refs = refs[1:]
    a_ref, qkv_ref, lse_ref, o_ref, part_ref = refs
    n = h.shape[0]
    width = wout_ref.shape[0]
    a = (h * inv_rms(h) * gain_ref[...]).astype(BF16)
    a_ref[...] = a
    lane = lax.broadcasted_iota(jnp.int32, (n, 2 * HD), 1)
    low_half = lane < HD
    zero = jnp.zeros((n, 2 * HD), BF16)
    mask = key_mask(open_ref, n)
    for t in range(width // (2 * HD)):
        spots = [slice(s * width + t * 2 * HD, s * width + (t + 1) * 2 * HD) for s in range(3)]
        q = rotate(mm(a, wqkv_ref[spots[0], :], NT), table_ref, 1)
        q = (q * HD ** (-0.5)).astype(BF16)
        k = rotate(mm(a, wqkv_ref[spots[1], :], NT), table_ref, 1).astype(BF16)
        v = mm(a, wqkv_ref[spots[2], :], NT).astype(BF16)
        qkv_ref[:, spots[0]] = q
        qkv_ref[:, spots[1]] = k
        qkv_ref[:, spots[2]] = v
        mixed = []
        for e in range(2):
            q_one = jnp.where(low_half if e == 0 else ~low_half, q, zero)
            s = jnp.where(mask, mm(k, q_one, NT), LOW)
            top = jnp.max(s, axis=0, keepdims=True)
            raised = jnp.exp(s - top)
            total = jnp.sum(raised, axis=0, keepdims=True)
            lse_ref[2 * t + e : 2 * t + e + 1, :] = top + jnp.log(total)
            prob = (raised / total).astype(BF16)
            mixed.append(mm(prob, v, TN))
        o_ref[:, t * 2 * HD : (t + 1) * 2 * HD] = jnp.where(low_half, mixed[0], mixed[1]).astype(BF16)
    part_ref[...] = mm(o_ref[...], wout_ref[...])


def ffn_fwd(h_ref, p_ref, r_ref, gain_ref, wgu_ref, wd_ref, h1_ref, b_ref, gu_ref, hid_ref, part_ref):
    h = h_ref[...] + (p_ref[...] + r_ref[...])
    h1_ref[...] = h
    b = (h * inv_rms(h) * gain_ref[...]).astype(BF16)
    b_ref[...] = b
    width = wd_ref.shape[0]
    step = min(width, 256)
    total = None
    for f in range(0, width, step):
        gate = mm(b, wgu_ref[0, :, f : f + step])
        up = mm(b, wgu_ref[1, :, f : f + step])
        gu_ref[:, f : f + step] = gate
        gu_ref[:, width + f : width + f + step] = up
        hid = (gate * jax.nn.sigmoid(gate) * up).astype(BF16)
        hid_ref[:, f : f + step] = hid
    part_ref[...] = mm(hid_ref[...], wd_ref[...])


def ffn_bwd(first, *refs):
    if first:
        g_ref, gu_ref, wgu_ref, wd_ref = refs[:4]
        refs = refs[4:]
        gm = g_ref[...]
    else:
        g1_ref, p_ref, r_ref, hin_ref, gain_ref, gu_ref, wgu_ref, wd_ref = refs[:8]
        refs = refs[8:]
        grad, gain_grad = close_norm(g1_ref[...], p_ref, r_ref, hin_ref, gain_ref)
        refs[0][...] = grad
        refs[1][...] = gain_grad
        gm = grad.astype(BF16)
        refs[2][...] = gm
        refs = refs[3:]
    dgu_ref, part_ref = refs
    width = wd_ref.shape[0]
    step = min(width, 256)
    for f in range(0, width, step):
        dhid = mm(gm, wd_ref[f : f + step, :], NT)
        gate = gu_ref[:, f : f + step]
        up = gu_ref[:, width + f : width + f + step]
        sig = jax.nn.sigmoid(gate)
        dgu_ref[:, f : f + step] = (dhid * up * (sig * (1.0 + gate * (1.0 - sig)))).astype(BF16)
        dgu_ref[:, width + f : width + f + step] = (dhid * (gate * sig)).astype(BF16)
    part_ref[...] = mm(dgu_ref[:, :width], wgu_ref[0], NT) + mm(dgu_ref[:, width:], wgu_ref[1], NT)


def close_norm(g, p_ref, r_ref, h_ref, gain_ref):
    grad = p_ref[...] + r_ref[...]
    h = h_ref[...]
    scale = inv_rms(h)
    normed = h * scale
    gain_grad = jnp.sum(grad * normed, axis=0, keepdims=True)
    return g + norm_back(grad, normed, scale, gain_ref[...]), gain_grad


def attn_bwd(
    g_ref, p_ref, r_ref, h1_ref, gain_ref, wqkv_ref, wout_ref, table_ref, open_ref, qkv_ref, lse_ref,
    g1_ref, gain_grad_ref, ga_ref, dqkv_ref, part_ref,
):
    g1, gain_grad = close_norm(g_ref[...].astype(F32), p_ref, r_ref, h1_ref, gain_ref)
    g1_ref[...] = g1
    gain_grad_ref[...] = gain_grad
    ga = g1.astype(BF16)
    ga_ref[...] = ga
    n = ga.shape[0]
    width = wout_ref.shape[0]
    lane = lax.broadcasted_iota(jnp.int32, (n, 2 * HD), 1)
    low_half = lane < HD
    zero = jnp.zeros((n, 2 * HD), BF16)
    mask = key_mask(open_ref, n)
    for t in range(width // (2 * HD)):
        spots = [slice(s * width + t * 2 * HD, s * width + (t + 1) * 2 * HD) for s in range(3)]
        q = qkv_ref[:, spots[0]]
        k = qkv_ref[:, spots[1]]
        v = qkv_ref[:, spots[2]]
        dout = mm(ga, wout_ref[t * 2 * HD : (t + 1) * 2 * HD, :], NT).astype(BF16)
        dq, dk, dv = [], [], []
        for e in range(2):
            mine = low_half if e == 0 else ~low_half
            q_one = jnp.where(mine, q, zero)
            d_one = jnp.where(mine, dout, zero)
            s = jnp.where(mask, mm(k, q_one, NT), LOW)
            prob = jnp.exp(s - lse_ref[2 * t + e : 2 * t + e + 1, :])
            dprob = mm(v, d_one, NT)
            delta = jnp.sum(prob * dprob, axis=0, keepdims=True)
            ds = (prob * (dprob - delta)).astype(BF16)
            dv.append(mm(prob.astype(BF16), dout))
            dk.append(mm(ds, q))
            dq.append(mm(ds, k, TN))
        dq = jnp.where(low_half, dq[0], dq[1]) * HD ** (-0.5)
        dk = jnp.where(low_half, dk[0], dk[1])
        dv = jnp.where(low_half, dv[0], dv[1])
        dqkv_ref[:, spots[0]] = rotate(dq, table_ref, -1).astype(BF16)
        dqkv_ref[:, spots[1]] = rotate(dk, table_ref, -1).astype(BF16)
        dqkv_ref[:, spots[2]] = dv.astype(BF16)
    part_ref[...] = mm(dqkv_ref[...], wqkv_ref[...])


def close_layer(g1_ref, p_ref, r_ref, h_ref, gain_ref, out_ref, gain_grad_ref):
    grad, gain_grad = close_norm(g1_ref[...], p_ref, r_ref, h_ref, gain_ref)
    out_ref[...] = grad
    gain_grad_ref[...] = gain_grad


def halves_of(half_ref, dim):
    one = dim // 2
    return [pl.ds(pl.multiple_of(half_ref[s] * one, one), one) for s in range(2)]


def grad_rows(spans, half_ref, *refs):
    chunks = (len(refs) - 2) // 2
    lefts, rights = refs[:chunks], refs[chunks : 2 * chunks]
    outs = refs[2 * chunks :]
    for s, spot in enumerate(halves_of(half_ref, rights[0].shape[1])):
        for out, picks in zip(outs, spans):
            at = 0
            for lo, hi in picks:
                total = None
                for left, right in zip(lefts, rights):
                    term = mm(left[:, lo:hi], right[:, spot], TN)
                    total = term if total is None else total + term
                out[s, at : at + hi - lo, :] = total
                at += hi - lo


def grad_columns(spans, half_ref, *refs):
    chunks = (len(refs) - 2) // 2
    lefts, rights = refs[:chunks], refs[chunks : 2 * chunks]
    outs = refs[2 * chunks :]
    for s, spot in enumerate(halves_of(half_ref, lefts[0].shape[1])):
        for out, picks in zip(outs, spans):
            at = 0
            for lo, hi in picks:
                total = None
                for left, right in zip(lefts, rights):
                    term = mm(left[:, spot], right[:, lo:hi], TN)
                    total = term if total is None else total + term
                out[s, :, at : at + hi - lo] = total
                at += hi - lo


def call(body, outs, args, flops, limit=40, smem=0):
    moved = sum(x.size * x.dtype.itemsize for x in args) + sum(
        int(np.prod(s)) * np.dtype(d).itemsize for s, d in outs
    )
    spec = pl.BlockSpec(memory_space=pltpu.VMEM)
    got = pl.pallas_call(
        body,
        out_shape=[jax.ShapeDtypeStruct(s, d) for s, d in outs],
        in_specs=[pl.BlockSpec(memory_space=pltpu.SMEM)] * smem + [spec] * (len(args) - smem),
        out_specs=[spec] * len(outs),
        compiler_params=pltpu.CompilerParams(vmem_limit_bytes=limit * 2**20),
        cost_estimate=pl.CostEstimate(flops=int(flops), bytes_accessed=int(moved), transcendentals=0),
    )(*args)
    return list(got)


def on_device(sizes, tokens, cotangent, heights, labels, valid, class_table, gains, w_qkv, w_out, w_gate_up, w_down):
    seq_count = heights.shape[0]
    row_count, dim = tokens.shape
    n = row_count // seq_count
    layers = gains.shape[0]
    classes = class_table.shape[0]
    la = w_out.shape[1]
    lf = w_down.shape[1]
    wa, wf = 2 * la, 2 * lf
    tp, dpo, dpi = sizes["tp"], sizes["dpo"], sizes["dpi"]
    mine = seq_count // 2
    core = lax.rem(lax.axis_index("tp"), 2)
    z = lax.axis_index("dpo")
    swap_core = [(i, i ^ 1) for i in range(tp)]

    def core_swap(x):
        return lax.ppermute(x, "tp", swap_core)

    def sum_chips(part):
        total = None
        for step in range(2, tp, 2):
            got = lax.ppermute(part, "tp", [(i, i ^ step) for i in range(tp)])
            total = got if total is None else total + got
        return total

    wqkv, wout, wgu, wd = [], [], [], []
    for l in range(layers):
        for into, w in (
            (wqkv, jnp.transpose(w_qkv[l], (1, 2, 0))),
            (wout, w_out[l][None]),
            (wgu, jnp.transpose(w_gate_up[l], (1, 0, 2))),
            (wd, w_down[l][None]),
        ):
            wide = w.astype(F32)
            axis = 2 if into is wgu else 1
            shape = list(w.shape)
            shape[axis] *= 2
            into.append(call(functools.partial(merge, axis), [(tuple(shape), BF16)], (wide, core_swap(wide)), 1000)[0])
        wqkv[l] = wqkv[l].reshape(3 * wa, dim)
        wout[l] = wout[l][0]
        wd[l] = wd[l][0]

    tables = jnp.asarray(rope_constants(n))
    position = jnp.arange(n)
    own = lambda x: lax.dynamic_slice_in_dim(x, core * mine, mine, 0)
    open_key = (position[None, :] < 1 + COLS * own(heights)[:, None]) & (own(valid.reshape(seq_count, n)) == 1)
    open_key = open_key.astype(F32)[:, :, None]
    own_labels = own(labels)
    token_own = own(tokens.reshape(seq_count, n, dim))
    cot_own = own(cotangent.reshape(seq_count, n, dim))
    chunks = range(mine)
    hs = []
    for c in chunks:
        row = lax.dynamic_slice_in_dim(class_table, own_labels[c], 1, 0)
        hs.append(jnp.where((position == 0)[:, None], row, token_own[c]).astype(F32))

    shape_d = ((n, dim), F32)
    shape_b = ((n, dim), BF16)
    flops_a = 2 * n * dim * 4 * wa + 8 * n * n * wa
    flops_f = 2 * n * dim * 3 * wf

    kept = []
    state = [(hs[c],) for c in chunks]
    parts = None
    for l in range(layers):
        keep = [dict() for _ in chunks]
        for c in chunks:
            args = state[c] + (gains[l, 0][None], wqkv[l], wout[l], tables, open_key[c])
            outs = [shape_b, ((n, 3 * wa), BF16), ((max(8, wa // HD), n), F32), ((n, wa), BF16), shape_d]
            if l > 0:
                outs = [shape_d] + outs
            got = call(functools.partial(attn_fwd, l == 0), outs, args, flops_a)
            h = state[c][0] if l == 0 else got.pop(0)
            a, qkv, lse, o, part = got
            keep[c].update(h=h, a=a, qkv=qkv, lse=lse, o=o)
            state[c] = (h, part, sum_chips(part))
        for c in chunks:
            args = state[c] + (gains[l, 1][None], wgu[l], wd[l])
            outs = [shape_d, shape_b, ((n, 2 * wf), F32), ((n, wf), BF16), shape_d]
            h1, b, gu, hid, part = call(ffn_fwd, outs, args, flops_f)
            keep[c].update(h1=h1, b=b, gu=gu, hid=hid)
            state[c] = (h1, part, sum_chips(part))
        kept.append(keep)

    output = jnp.concatenate([s[0] + (s[1] + s[2]) for s in state], axis=0)

    half = lax.axis_index("dpi") if dpi == 2 else 1
    order = jnp.stack([jnp.int32(1) - half, jnp.int32(half)])

    def dp_sum(both, other, axis):
        got = core_swap(other)
        if dpi == 2:
            sent = lax.ppermute(both[0] + got[0], "dpi", [(0, 1), (1, 0)])
            total = (both[1] + got[1]) + sent
        else:
            both = both + got
            whole = jnp.concatenate([both[0], both[1]], axis=axis)
            total = lax.psum_scatter(whole, "dpi", scatter_dimension=axis, tiled=True)
        return line_sum(total)

    def line_sum(x):
        if dpo != 4:
            return lax.psum(x, "dpo")
        got = lax.ppermute(x, "dpo", [(0, 1), (3, 2)])
        x = x + got
        got = lax.ppermute(x, "dpo", [(1, 2), (2, 1)])
        x = x + got
        got = lax.ppermute(x, "dpo", [(1, 0), (2, 3)])
        return jnp.where((z == 0) | (z == dpo - 1), got, x)

    gain_rows = [[None, None] for _ in range(layers)]
    grads = [None] * layers
    state = [None] * mine
    for l in reversed(range(layers)):
        top = l == layers - 1
        keep = kept[l]
        gms = []
        for c in chunks:
            outs = [((n, 2 * wf), BF16), shape_d]
            args = (keep[c]["gu"], wgu[l], wd[l])
            if top:
                g = cot_own[c]
                dgu, part = call(functools.partial(ffn_bwd, True), outs, (g,) + args, flops_f)
                gms.append(g)
            else:
                outs = [shape_d, ((1, dim), F32), shape_b] + outs
                args = state[c] + args
                g, gain_c, gm, dgu, part = call(functools.partial(ffn_bwd, False), outs, args, flops_f)
                gain_rows[l + 1][0] = gain_c if c == 0 else gain_rows[l + 1][0] + gain_c
                gms.append(gm)
            keep[c]["dgu"] = dgu
            state[c] = (g, part, sum_chips(part), keep[c]["h1"], gains[l, 1][None])
        flops_w = 2 * n * mine * dim * wf
        outs = [((2, lf, dim // 2), F32)] * 2
        args = [order] + [keep[c]["hid"] for c in chunks] + gms
        spans = (((0, lf),), ((lf, wf),))
        down = call(functools.partial(grad_rows, spans), outs, args, flops_w, smem=1)
        outs = [((2, dim // 2, 2 * lf), F32)] * 2
        args = [order] + [keep[c]["b"] for c in chunks] + [keep[c]["dgu"] for c in chunks]
        spans = (((0, lf), (wf, wf + lf)), ((lf, wf), (wf + lf, 2 * wf)))
        gate_up = call(functools.partial(grad_columns, spans), outs, args, 2 * flops_w, smem=1)
        down = dp_sum(*down, 1)
        gate_up = dp_sum(*gate_up, 0)
        gas = []
        for c in chunks:
            outs = [shape_d, ((1, dim), F32), shape_b, ((n, 3 * wa), BF16), shape_d]
            args = state[c] + (wqkv[l], wout[l], tables, open_key[c], keep[c]["qkv"], keep[c]["lse"])
            g1, gain_c, ga, dqkv, part = call(attn_bwd, outs, args, flops_a + 12 * n * n * wa)
            gain_rows[l][1] = gain_c if c == 0 else gain_rows[l][1] + gain_c
            gas.append(ga)
            keep[c]["dqkv"] = dqkv
            state[c] = (g1, part, sum_chips(part), keep[c]["h"], gains[l, 0][None])
        flops_w = 2 * n * mine * dim * wa
        outs = [((2, la, dim // 2), F32)] * 2
        args = [order] + [keep[c]["o"] for c in chunks] + gas
        spans = (((0, la),), ((la, wa),))
        out = call(functools.partial(grad_rows, spans), outs, args, flops_w, smem=1)
        outs = [((2, 3 * la, dim // 2), F32)] * 2
        args = [order] + [keep[c]["dqkv"] for c in chunks] + [keep[c]["a"] for c in chunks]
        spans = tuple(tuple((t * wa + s * la, t * wa + (s + 1) * la) for t in range(3)) for s in range(2))
        qkv = call(functools.partial(grad_rows, spans), outs, args, 3 * flops_w, smem=1)
        out = dp_sum(*out, 1)
        qkv = dp_sum(*qkv, 1)
        grads[l] = (qkv, out, gate_up, down)

    finals = []
    for c in chunks:
        g, gain_c = call(close_layer, [shape_d, ((1, dim), F32)], state[c], 1000)
        gain_rows[0][0] = gain_c if c == 0 else gain_rows[0][0] + gain_c
        finals.append(g)

    slot0 = lax.axis_index("dpo") * dpi + lax.axis_index("dpi")
    seqs = seq_count * dpo * dpi
    firsts = jnp.concatenate([g[0:1] for g in finals], axis=0)
    small = jnp.zeros((seqs + 2 * layers + 1, dim), F32)
    small = lax.dynamic_update_slice(small, firsts, (slot0 * seq_count + core * mine, 0))
    terms = jnp.concatenate([gain_rows[l][i] for l in range(layers) for i in range(2)], axis=0)
    small = lax.dynamic_update_slice(small, terms, (seqs, 0))
    label_row = lax.dynamic_update_slice(
        jnp.zeros((1, dim), F32), own_labels.astype(F32)[None], (0, slot0 * seq_count + core * mine)
    )
    small = lax.dynamic_update_slice(small, label_row, (seqs + 2 * layers, 0))
    small = jnp.where(lax.axis_index("tp") < 2, small, 0.0)
    small = lax.psum(small, ("dpo", "dpi", "tp"))
    all_labels = jnp.round(small[seqs + 2 * layers, :seqs]).astype(jnp.int32)
    gain_total = small[seqs : seqs + 2 * layers].reshape(layers, 2, dim)
    onehot = (all_labels[None, :] == jnp.arange(classes)[:, None]).astype(F32)
    share = dim // dpi
    rows = lax.dynamic_slice(small, (0, lax.axis_index("dpi") * share), (seqs, share))
    table_part = jnp.dot(onehot, rows, precision=lax.Precision.HIGHEST)

    token_own = jnp.concatenate([jnp.where((position == 0)[:, None], 0.0, g) for g in finals], axis=0)

    def both_cores(x):
        other = core_swap(x)
        return jnp.where(core == 0, jnp.concatenate([x, other], 0), jnp.concatenate([other, x], 0))

    qkv_part = jnp.stack([g[0].reshape(3, la, share) for g in grads]).transpose(0, 3, 1, 2)
    out_part = jnp.stack([g[1] for g in grads])
    gate_up_part = jnp.stack([g[2].reshape(share, 2, lf) for g in grads])
    down_part = jnp.stack([g[3] for g in grads])
    return (
        both_cores(output),
        both_cores(token_own),
        table_part,
        gain_total,
        qkv_part,
        out_part,
        gate_up_part,
        down_part,
    )


def solution(mesh):
    sizes = dict(mesh.shape)
    placed = (
        P(("dpo", "dpi"), None),
        P(("dpo", "dpi"), None),
        P(("dpo", "dpi")),
        P(("dpo", "dpi")),
        P(("dpo", "dpi")),
        P(),
        P(),
        P(None, None, None, "tp"),
        P(None, "tp", None),
        P(None, None, None, "tp"),
        P(None, "tp", None),
    )
    return jax.shard_map(
        functools.partial(on_device, sizes),
        mesh=mesh,
        in_specs=placed,
        out_specs=(
            P(("dpo", "dpi"), None),
            P(("dpo", "dpi"), None),
            P(None, "dpi"),
            P(),
            P(None, "dpi", None, "tp"),
            P(None, "tp", "dpi"),
            P(None, "dpi", None, "tp"),
            P(None, "tp", "dpi"),
        ),
        check_vma=False,
    )
```

time: 1270 us -> 861 us (0.68)
  waiting for transfers between devices: 980 us -> 488 us
  Pallas kernels: 0 us -> 96 us
  starting transfers between devices: 1.8 us -> 94.3 us
  matrix products: 84.6 us -> 2.09 us
  blocking collectives: 43.3 us -> 0 us
  other arithmetic: 63.3 us -> 86.4 us
    psum x8 -> x1, waiting for transfers between devices: 763 us -> 119 us  [on_device(): small = lax.psum(small, ('dpo', 'dpi', 'tp'))]
    ppermute x0 -> x66, waiting for transfers between devices: none -> 369 us  [the longest x16 129 us: sum_chips(): got = lax.ppermute(part, 'tp', [(i, i ^ step) for i in range(tp)])]
    reduce_scatter x5 -> x0, waiting for transfers between devices: 216 us -> none  [the longest x1 79.3 us: on_device(): lax.psum_scatter(gate_up_all, 'dpi', scatter_dimension=1, tiled=True)]
    pallas_call x0 -> x34, Pallas kernels: none -> 96 us  [call(): pl.pallas_call(body, out_shape=[jax.ShapeDtypeStruct(s, d) for s, d in ou...]
    ppermute x0 -> x66, starting transfers between devices: none -> 94.3 us  [the longest x8 30.2 us: line_sum(): got = lax.ppermute(x, 'dpo', [(0, 1), (3, 2)])]
    dot_general x36 -> x1, matrix products: 80.9 us -> 2.09 us  [on_device(): table_part = jnp.dot(onehot, rows, precision=lax.Precision.HIGHEST)]
    psum x1 -> x0, blocking collectives: 43.3 us -> none  [on_device(): gain_total = lax.psum(gain_all, ('dpo', 'dpi', 'tp'))]
    add x7 -> x38, other arithmetic: 7.42 us -> 47 us  [the longest x16 25 us: line_sum(): x = x + got]
  transfers between devices with their start and end apart: 13 -> 67, of which waited for: 12 -> 29; matrix products, arithmetic and copies ran while one was open for 4% -> 11% of each run, Pallas kernels for 0% -> 10%
where the time goes in v1:
time: 861 us; the launch traced here: 850 us
  waiting for transfers between devices  488 us (57%)
  Pallas kernels  96 us (11%)
  starting transfers between devices  94.3 us (11%)
  other arithmetic  86.4 us (10%)
  local copies, waits for them, and re-layouts  62.3 us (7%)
  between operations  20.1 us (2%)
    ppermute x16, waiting for transfers between devices, sum_chips(): got = lax.ppermute(part, 'tp', [(i, i ^ step) for i in range(tp)])  129 us
    psum x1, waiting for transfers between devices, on_device(): small = lax.psum(small, ('dpo', 'dpi', 'tp'))  119 us
    ppermute x8, waiting for transfers between devices, line_sum(): got = lax.ppermute(x, 'dpo', [(1, 0), (2, 3)])  113 us
    pallas_call x34, Pallas kernels, call(): pl.pallas_call(body, out_shape=[jax.ShapeDtypeStruct(s, d) for s, d in ou...  96 us
    ppermute x8, waiting for transfers between devices, dp_sum(): sent = lax.ppermute(both[0] + got[0], 'dpi', [(0, 1), (1, 0)])  64.9 us
    ppermute x8, waiting for transfers between devices, line_sum(): got = lax.ppermute(x, 'dpo', [(0, 1), (3, 2)])  62.1 us
    unnamed x378, local copies, waits for them, and re-layouts  46.8 us
    ppermute x8, starting transfers between devices, line_sum(): got = lax.ppermute(x, 'dpo', [(0, 1), (3, 2)])  30.2 us
  transfers between devices with their start and end apart: 67, of which 29 were waited for; matrix products, arithmetic and copies ran while one was open for 11% of the time, Pallas kernels for 10%

profile of v1, /device:TPU:0, one launch (start us, length us, event | category | flops | bytes accessed | tf_op | source)
XLA Modules:
  0.0 849.6 jit_solution(10438478539532322585)
XLA Ops:
  37.0 4.5 shard_map.181
  73.9 8.6 %collective-permute-done.12.r_ref = f32[256,768]{1,0:T(8,128)S(1)} collective-permute-done((f32[256,768]{1,0:T(8,128)S(1)}, f32[256,768]{1,0:T(8,128)S(1)}, u32[]{:S(2)}, u32[]{:S(2)}) %collective-permute-start.12) | collective-permute-done | bytes 786464 | tf_op jit(solution)/shard_map/ppermute | solution.py:295
  90.3 9.1 %collective-permute-done.5.refs_2_ = f32[256,768]{1,0:T(8,128)S(1)} collective-permute-done((f32[256,768]{1,0:T(8,128)S(1)}, f32[256,768]{1,0:T(8,128)S(1)}, u32[]{:S(2)}, u32[]{:S(2)}) %collective-permute-start.5) | collective-permute-done | bytes 786464 | tf_op jit(solution)/shard_map/ppermute | solution.py:295
  108.3 7.9 collective-permute-done.13.refs_2_
  126.3 6.8 collective-permute-done.8.r_ref
  143.5 6.4 collective-permute-done.14.r_ref
  159.4 7.5 collective-permute-done.17.r_ref
  174.2 5.7 shard_map.196
  183.5 6.6 shard_map.201
  204.0 8.8 %collective-permute-done.18.refs_2_ = f32[256,768]{1,0:T(8,128)S(1)} collective-permute-done((f32[256,768]{1,0:T(8,128)S(1)}, f32[256,768]{1,0:T(8,128)S(1)}, u32[]{:S(2)}, u32[]{:S(2)}) %collective-permute-start.18) | collective-permute-done | bytes 786464 | tf_op jit(solution)/shard_map/ppermute | solution.py:295
  224.3 5.5 collective-permute-done.22.refs_2_
  239.3 7.3 collective-permute-done.11
  251.3 11.7 %collective-permute-done.15 = f32[256,768]{1,0:T(8,128)} collective-permute-done((f32[256,768]{1,0:T(8,128)}, f32[256,768]{1,0:T(8,128)}, u32[]{:S(2)}, u32[]{:S(2)}) %collective-permute-start.15) | collective-permute-done | bytes 786464 | tf_op jit(solution)/shard_map/ppermute | solution.py:295
  268.3 4.4 collective-permute-done.43
  279.1 8.2 collective-permute-done.19.r_ref
  287.4 15.1 %collective-permute-done.23.r_ref = f32[256,768]{1,0:T(8,128)S(1)} collective-permute-done((f32[256,768]{1,0:T(8,128)S(1)}, f32[256,768]{1,0:T(8,128)S(1)}, u32[]{:S(2)}, u32[]{:S(2)}) %collective-permute-start.23) | collective-permute-done | bytes 786464 | tf_op jit(solution)/shard_map/ppermute | solution.py:295
  308.3 4.2 shard_map.198
  332.1 13.8 %collective-permute-done.62 = f32[512,384]{1,0:T(8,128)S(1)} collective-permute-done((f32[512,384]{1,0:T(8,128)S(1)}, f32[512,384]{1,0:T(8,128)S(1)}, u32[]{:S(2)}, u32[]{:S(2)}) %collective-permute-start.62) | collective-permute-done | bytes 786464 | tf_op jit(solution)/shard_map/ppermute | solution.py:366
  353.8 51.0 %collective-permute-done.37 = f32[192,384]{1,0:T(8,128)S(1)} collective-permute-done((f32[192,384]{1,0:T(8,128)S(1)}, f32[192,384]{1,0:T(8,128)S(1)}, u32[]{:S(2)}, u32[]{:S(2)}) %collective-permute-start.37) | collective-permute-done | bytes 294944 | tf_op jit(solution)/shard_map/ppermute | solution.py:366
  414.5 10.9 %collective-permute-done.20.r_ref = f32[256,768]{1,0:T(8,128)S(1)} collective-permute-done((f32[256,768]{1,0:T(8,128)S(1)}, f32[256,768]{1,0:T(8,128)S(1)}, u32[]{:S(2)}, u32[]{:S(2)}) %collective-permute-start.20) | collective-permute-done | bytes 786464 | tf_op jit(solution)/shard_map/ppermute | solution.py:295
  430.7 8.9 %collective-permute-done.24.r_ref = f32[256,768]{1,0:T(8,128)S(1)} collective-permute-done((f32[256,768]{1,0:T(8,128)S(1)}, f32[256,768]{1,0:T(8,128)S(1)}, u32[]{:S(2)}, u32[]{:S(2)}) %collective-permute-start.24) | collective-permute-done | bytes 786464 | tf_op jit(solution)/shard_map/ppermute | solution.py:295
  449.2 22.5 %collective-permute-done.38 = f32[192,384]{1,0:T(8,128)S(1)} collective-permute-done((f32[192,384]{1,0:T(8,128)S(1)}, f32[192,384]{1,0:T(8,128)S(1)}, u32[]{:S(2)}, u32[]{:S(2)}) %collective-permute-start.38) | collective-permute-done | bytes 294944 | tf_op jit(solution)/shard_map/ppermute | solution.py:377
  471.7 5.5 collective-permute-start.48
  482.0 8.6 %collective-permute-done.33 = f32[576,384]{1,0:T(8,128)S(1)} collective-permute-done((f32[576,384]{1,0:T(8,128)S(1)}, f32[576,384]{1,0:T(8,128)S(1)}, u32[]{:S(2)}, u32[]{:S(2)}) %collective-permute-start.33) | collective-permute-done | bytes 884768 | tf_op jit(solution)/shard_map/ppermute | solution.py:377
  492.0 6.3 collective-permute-start.58
  514.7 26.6 %collective-permute-done.58 = f32[512,384]{1,0:T(8,128)} collective-permute-done((f32[512,384]{1,0:T(8,128)}, f32[512,384]{1,0:T(8,128)}, u32[]{:S(2)}, u32[]{:S(2)}) %collective-permute-start.58) | collective-permute-done | bytes 786464 | tf_op jit(solution)/shard_map/ppermute | solution.py:377
  564.8 119.2 %all-reduce.2.cloned.1.call-done = f32[37,768]{1,0:T(8,128)} async-done(((f32[37,768]{1,0:T(8,128)}), f32[37,768]{1,0:T(8,128)}) %all-reduce.2.cloned.1.call-update) | async-done | bytes 113680 | tf_op jit(solution)/shard_map/psum | solution.py:457
  715.0 16.2 %collective-permute-done.35 = f32[576,384]{1,0:T(8,128)} collective-permute-done((f32[576,384]{1,0:T(8,128)}, f32[576,384]{1,0:T(8,128)}, u32[]{:S(2)}, u32[]{:S(2)}) %collective-permute-start.35) | collective-permute-done | bytes 884768 | tf_op jit(solution)/shard_map/ppermute | solution.py:381
  732.5 15.5 %collective-permute-done.60 = f32[512,384]{1,0:T(8,128)S(1)} collective-permute-done((f32[512,384]{1,0:T(8,128)S(1)}, f32[512,384]{1,0:T(8,128)S(1)}, u32[]{:S(2)}, u32[]{:S(2)}) %collective-permute-start.60) | collective-permute-done | bytes 786464 | tf_op jit(solution)/shard_map/ppermute | solution.py:381
  749.3 51.3 %collective-permute-done.30 = f32[576,384]{1,0:T(8,128)S(1)} collective-permute-done((f32[576,384]{1,0:T(8,128)S(1)}, f32[576,384]{1,0:T(8,128)S(1)}, u32[]{:S(2)}, u32[]{:S(2)}) %collective-permute-start.30) | collective-permute-done | bytes 884768 | tf_op jit(solution)/shard_map/ppermute | solution.py:381
  804.9 28.9 %collective-permute-done.50 = f32[384,1024]{1,0:T(8,128)} collective-permute-done((f32[384,1024]{1,0:T(8,128)S(1)}, f32[384,1024]{1,0:T(8,128)}, u32[]{:S(2)}, u32[]{:S(2)}) %collective-permute-start.50) | collective-permute-done | bytes 1572896 | tf_op jit(solution)/shard_map/ppermute | solution.py:381
  838.0 4.5 pad_maximum_fusion
  (606 shorter events, 311.4 us)
Async XLA Ops:
  7.2 676.8 %all-reduce.2.cloned.1.call-start = ((), (), s32[]{:S(2)}) async-start(), calls=%async_computation | async-start | bytes 245760 | tf_op jit(solution)/shard_map/psum | solution.py:457
  21.3 101.8 %collective-permute-start.9 = (f32[2,768,512]{2,1,0:T(8,128)}, f32[2,768,512]{2,1,0:T(8,128)}, u32[]{:S(2)}, u32[]{:S(2)}) collective-permute-start(f32[2,768,512]{2,1,0:T(8,128)} %convert_bitcast_fusion.mine_ref), channel_id=1, source_target_pairs={{0,1},{1,0},{2,3},{3,2},{4,5},{5,4},{6,7},{7,6},{8,9},{9,8},{10,11... | collective-permute-start | bytes 9437192 | tf_op jit(solution)/shard_map/ppermute | solution.py:290
  29.6 58.2 %collective-permute-start.6 = (f32[3,192,768]{2,1,0:T(8,128)}, f32[3,192,768]{2,1,0:T(8,128)}, u32[]{:S(2)}, u32[]{:S(2)}) collective-permute-start(f32[3,192,768]{2,1,0:T(8,128)} %get-tuple-element.206.mine_ref), channel_id=1, source_target_pairs={{0,1},{1,0},{2,3},{3,2},{4,5},{5,4},{6,7},{7,6},{8,9},{9,8},{10,11... | collective-permute-start | bytes 5308424 | tf_op jit(solution)/shard_map/ppermute | solution.py:290
  198.6 126.8 %collective-permute-start.51 = (f32[2,384,1024]{2,1,0:T(8,128)}, f32[2,384,1024]{2,1,0:T(8,128)}, u32[]{:S(2)}, u32[]{:S(2)}) collective-permute-start(f32[2,384,1024]{2,1,0:T(8,128)} %get-tuple-element.189), channel_id=1, source_target_pairs={{0,1},{1,0},{2,3},{3,2},{4,5},{5,4},{6,7},{7,6},{8,9},{9,8},{10,11... | collective-permute-start | bytes 9437192 | tf_op jit(solution)/shard_map/ppermute | solution.py:290
  201.7 65.1 %collective-permute-start.61 = (f32[2,512,384]{2,1,0:T(8,128)S(1)}, f32[2,512,384]{2,1,0:T(8,128)}, u32[]{:S(2)}, u32[]{:S(2)}) collective-permute-start(f32[2,512,384]{2,1,0:T(8,128)S(1)} %get-tuple-element.199), channel_id=1, source_target_pairs={{0,1},{1,0},{2,3},{3,2},{4,5},{5,4},{6,7},{7,6},{8,9},{9,8},{10,11... | collective-permute-start | bytes 4718600 | tf_op jit(solution)/shard_map/ppermute | solution.py:290
  202.2 44.4 %collective-permute-start.11 = (f32[256,768]{1,0:T(8,128)}, f32[256,768]{1,0:T(8,128)}, u32[]{:S(2)}, u32[]{:S(2)}) collective-permute-start(f32[256,768]{1,0:T(8,128)} %get-tuple-element.110), channel_id=1, source_target_pairs={{0,2},{1,3},{2,0},{3,1},{4,6},{5,7},{6,4},{7,5},{8,10},{9,11},{10,... | collective-permute-start | bytes 2359304 | tf_op jit(solution)/shard_map/ppermute | solution.py:295
  213.7 49.3 %collective-permute-start.15 = (f32[256,768]{1,0:T(8,128)}, f32[256,768]{1,0:T(8,128)}, u32[]{:S(2)}, u32[]{:S(2)}) collective-permute-start(f32[256,768]{1,0:T(8,128)} %get-tuple-element.117), channel_id=1, source_target_pairs={{0,2},{1,3},{2,0},{3,1},{4,6},{5,7},{6,4},{7,5},{8,10},{9,11},{10,... | collective-permute-start | bytes 2359304 | tf_op jit(solution)/shard_map/ppermute | solution.py:295
  246.6 99.3 %collective-permute-start.46 = (f32[2,384,1024]{2,1,0:T(8,128)}, f32[2,384,1024]{2,1,0:T(8,128)}, u32[]{:S(2)}, u32[]{:S(2)}) collective-permute-start(f32[2,384,1024]{2,1,0:T(8,128)} %get-tuple-element.183), channel_id=1, source_target_pairs={{0,1},{1,0},{2,3},{3,2},{4,5},{5,4},{6,7},{7,6},{8,9},{9,8},{10,11... | collective-permute-start | bytes 9437192 | tf_op jit(solution)/shard_map/ppermute | solution.py:290
  250.8 69.0 %collective-permute-start.31 = (f32[2,576,384]{2,1,0:T(8,128)}, f32[2,576,384]{2,1,0:T(8,128)}, u32[]{:S(2)}, u32[]{:S(2)}) collective-permute-start(f32[2,576,384]{2,1,0:T(8,128)} %get-tuple-element.165), channel_id=1, source_target_pairs={{0,1},{1,0},{2,3},{3,2},{4,5},{5,4},{6,7},{7,6},{8,9},{9,8},{10,11... | collective-permute-start | bytes 5308424 | tf_op jit(solution)/shard_map/ppermute | solution.py:290
  287.3 43.3 %collective-permute-start.16 = (f32[512,768]{1,0:T(8,128)}, f32[512,768]{1,0:T(8,128)}, u32[]{:S(2)}, u32[]{:S(2)}) collective-permute-start(f32[512,768]{1,0:T(8,128)} %pad_maximum_fusion.1), channel_id=1, source_target_pairs={{0,1},{1,0},{2,3},{3,2},{4,5},{5,4},{6,7},{7,6},{8,9},{9,8},{10,11... | collective-permute-start | bytes 4718600 | tf_op jit(solution)/shard_map/ppermute | solution.py:290
  328.7 78.4 %collective-permute-start.52 = (f32[384,1024]{1,0:T(8,128)S(1)}, f32[384,1024]{1,0:T(8,128)S(1)}, u32[]{:S(2)}, u32[]{:S(2)}) collective-permute-start(f32[384,1024]{1,0:T(8,128)S(1)} %fusion), channel_id=1, source_target_pairs={{0,4},{4,0},{1,5},{5,1},{2,6},{6,2},{3,7},{7,3},{8,12},{12,8},{9,1... | collective-permute-start | bytes 4718600 | tf_op jit(solution)/shard_map/ppermute | solution.py:366
  345.9 81.0 %collective-permute-start.26 = (f32[2,576,384]{2,1,0:T(8,128)S(1)}, f32[2,576,384]{2,1,0:T(8,128)S(1)}, u32[]{:S(2)}, u32[]{:S(2)}) collective-permute-start(f32[2,576,384]{2,1,0:T(8,128)S(1)} %get-tuple-element.159), channel_id=1, source_target_pairs={{0,1},{1,0},{2,3},{3,2},{4,5},{5,4},{6,7},{7,6},{8,9},{9,8},{10,11... | collective-permute-start | bytes 5308424 | tf_op jit(solution)/shard_map/ppermute | solution.py:290
  345.9 60.6 %collective-permute-start.32 = (f32[576,384]{1,0:T(8,128)S(1)}, f32[576,384]{1,0:T(8,128)S(1)}, u32[]{:S(2)}, u32[]{:S(2)}) collective-permute-start(f32[576,384]{1,0:T(8,128)S(1)} %fusion.6), channel_id=1, source_target_pairs={{0,4},{4,0},{1,5},{5,1},{2,6},{6,2},{3,7},{7,3},{8,12},{12,8},{9,1... | collective-permute-start | bytes 2654216 | tf_op jit(solution)/shard_map/ppermute | solution.py:366
  349.1 55.8 %collective-permute-start.37 = (f32[192,384]{1,0:T(8,128)S(1)}, f32[192,384]{1,0:T(8,128)S(1)}, u32[]{:S(2)}, u32[]{:S(2)}) collective-permute-start(f32[192,384]{1,0:T(8,128)S(1)} %fusion.26), channel_id=1, source_target_pairs={{0,4},{4,0},{1,5},{5,1},{2,6},{6,2},{3,7},{7,3},{8,12},{12,8},{9,1... | collective-permute-start | bytes 884744 | tf_op jit(solution)/shard_map/ppermute | solution.py:366
  349.7 94.9 %collective-permute-start.47 = (f32[384,1024]{1,0:T(8,128)S(1)}, f32[384,1024]{1,0:T(8,128)S(1)}, u32[]{:S(2)}, u32[]{:S(2)}) collective-permute-start(f32[384,1024]{1,0:T(8,128)S(1)} %fusion.3), channel_id=1, source_target_pairs={{0,4},{4,0},{1,5},{5,1},{2,6},{6,2},{3,7},{7,3},{8,12},{12,8},{9,1... | collective-permute-start | bytes 4718600 | tf_op jit(solution)/shard_map/ppermute | solution.py:366
  425.4 52.8 %collective-permute-start.57 = (f32[512,384]{1,0:T(8,128)S(1)}, f32[512,384]{1,0:T(8,128)S(1)}, u32[]{:S(2)}, u32[]{:S(2)}) collective-permute-start(f32[512,384]{1,0:T(8,128)S(1)} %fusion.15), channel_id=1, source_target_pairs={{0,4},{4,0},{1,5},{5,1},{2,6},{6,2},{3,7},{7,3},{8,12},{12,8},{9,1... | collective-permute-start | bytes 2359304 | tf_op jit(solution)/shard_map/ppermute | solution.py:366
  426.9 72.5 %collective-permute-start.53 = (f32[384,1024]{1,0:T(8,128)S(1)}, f32[384,1024]{1,0:T(8,128)S(1)}, u32[]{:S(2)}, u32[]{:S(2)}) collective-permute-start(f32[384,1024]{1,0:T(8,128)S(1)} %fusion.2), channel_id=1, source_target_pairs={{0,8},{24,16},{1,9},{25,17},{2,10},{26,18},{3,11},{27,19},{4,12},{... | collective-permute-start | bytes 4718600 | tf_op jit(solution)/shard_map/ppermute | solution.py:377
  443.3 47.4 %collective-permute-start.33 = (f32[576,384]{1,0:T(8,128)S(1)}, f32[576,384]{1,0:T(8,128)S(1)}, u32[]{:S(2)}, u32[]{:S(2)}) collective-permute-start(f32[576,384]{1,0:T(8,128)S(1)} %fusion.8), channel_id=1, source_target_pairs={{0,8},{24,16},{1,9},{25,17},{2,10},{26,18},{3,11},{27,19},{4,12},{... | collective-permute-start | bytes 2654216 | tf_op jit(solution)/shard_map/ppermute | solution.py:377
  444.6 47.4 %collective-permute-start.27 = (f32[576,384]{1,0:T(8,128)S(1)}, f32[576,384]{1,0:T(8,128)S(1)}, u32[]{:S(2)}, u32[]{:S(2)}) collective-permute-start(f32[576,384]{1,0:T(8,128)S(1)} %fusion.9), channel_id=1, source_target_pairs={{0,4},{4,0},{1,5},{5,1},{2,6},{6,2},{3,7},{7,3},{8,12},{12,8},{9,1... | collective-permute-start | bytes 2654216 | tf_op jit(solution)/shard_map/ppermute | solution.py:366
  471.7 69.6 %collective-permute-start.48 = (f32[384,1024]{1,0:T(8,128)}, f32[384,1024]{1,0:T(8,128)}, u32[]{:S(2)}, u32[]{:S(2)}) collective-permute-start(f32[384,1024]{1,0:T(8,128)} %fusion.5), channel_id=1, source_target_pairs={{0,8},{24,16},{1,9},{25,17},{2,10},{26,18},{3,11},{27,19},{4,12},{... | collective-permute-start | bytes 4718600 | tf_op jit(solution)/shard_map/ppermute | solution.py:377
  492.0 49.3 %collective-permute-start.58 = (f32[512,384]{1,0:T(8,128)}, f32[512,384]{1,0:T(8,128)}, u32[]{:S(2)}, u32[]{:S(2)}) collective-permute-start(f32[512,384]{1,0:T(8,128)} %fusion.17), channel_id=1, source_target_pairs={{0,8},{24,16},{1,9},{25,17},{2,10},{26,18},{3,11},{27,19},{4,12},{... | collective-permute-start | bytes 2359304 | tf_op jit(solution)/shard_map/ppermute | solution.py:377
  500.5 54.1 %collective-permute-start.28 = (f32[576,384]{1,0:T(8,128)}, f32[576,384]{1,0:T(8,128)}, u32[]{:S(2)}, u32[]{:S(2)}) collective-permute-start(f32[576,384]{1,0:T(8,128)} %fusion.11), channel_id=1, source_target_pairs={{0,8},{24,16},{1,9},{25,17},{2,10},{26,18},{3,11},{27,19},{4,12},{... | collective-permute-start | bytes 2654216 | tf_op jit(solution)/shard_map/ppermute | solution.py:377
  508.2 54.3 %collective-permute-start.34 = (f32[576,384]{1,0:T(8,128)}, f32[576,384]{1,0:T(8,128)}, u32[]{:S(2)}, u32[]{:S(2)}) collective-permute-start(f32[576,384]{1,0:T(8,128)} %add.256), channel_id=1, source_target_pairs={{8,16},{16,8},{9,17},{17,9},{10,18},{18,10},{11,19},{19,11},{12,20... | collective-permute-start | bytes 2654216 | tf_op jit(solution)/shard_map/ppermute | solution.py:379
  509.7 181.2 %collective-permute-start.54 = (f32[384,1024]{1,0:T(8,128)S(1)}, f32[384,1024]{1,0:T(8,128)}, u32[]{:S(2)}, u32[]{:S(2)}) collective-permute-start(f32[384,1024]{1,0:T(8,128)S(1)} %add.284), channel_id=1, source_target_pairs={{8,16},{16,8},{9,17},{17,9},{10,18},{18,10},{11,19},{19,11},{12,20... | collective-permute-start | bytes 4718600 | tf_op jit(solution)/shard_map/ppermute | solution.py:379
  541.3 158.7 %collective-permute-start.25 = (f32[512,768]{1,0:T(8,128)}, f32[512,768]{1,0:T(8,128)}, u32[]{:S(2)}, u32[]{:S(2)}) collective-permute-start(f32[512,768]{1,0:T(8,128)} %pad_maximum_fusion.2), channel_id=1, source_target_pairs={{0,1},{1,0},{2,3},{3,2},{4,5},{5,4},{6,7},{7,6},{8,9},{9,8},{10,11... | collective-permute-start | bytes 4718600 | tf_op jit(solution)/shard_map/ppermute | solution.py:290
  553.0 136.5 %collective-permute-start.59 = (f32[512,384]{1,0:T(8,128)}, f32[512,384]{1,0:T(8,128)}, u32[]{:S(2)}, u32[]{:S(2)}) collective-permute-start(f32[512,384]{1,0:T(8,128)} %add.291), channel_id=1, source_target_pairs={{8,16},{16,8},{9,17},{17,9},{10,18},{18,10},{11,19},{19,11},{12,20... | collective-permute-start | bytes 2359304 | tf_op jit(solution)/shard_map/ppermute | solution.py:379
  554.6 153.5 %collective-permute-start.49 = (f32[384,1024]{1,0:T(8,128)}, f32[384,1024]{1,0:T(8,128)}, u32[]{:S(2)}, u32[]{:S(2)}) collective-permute-start(f32[384,1024]{1,0:T(8,128)} %add.277), channel_id=1, source_target_pairs={{8,16},{16,8},{9,17},{17,9},{10,18},{18,10},{11,19},{19,11},{12,20... | collective-permute-start | bytes 4718600 | tf_op jit(solution)/shard_map/ppermute | solution.py:379
  562.5 138.9 %collective-permute-start.29 = (f32[576,384]{1,0:T(8,128)}, f32[576,384]{1,0:T(8,128)}, u32[]{:S(2)}, u32[]{:S(2)}) collective-permute-start(f32[576,384]{1,0:T(8,128)} %add.249), channel_id=1, source_target_pairs={{8,16},{16,8},{9,17},{17,9},{10,18},{18,10},{11,19},{19,11},{12,20... | collective-permute-start | bytes 2654216 | tf_op jit(solution)/shard_map/ppermute | solution.py:379
  700.0 47.9 %collective-permute-start.60 = (f32[512,384]{1,0:T(8,128)S(1)}, f32[512,384]{1,0:T(8,128)S(1)}, u32[]{:S(2)}, u32[]{:S(2)}) collective-permute-start(f32[512,384]{1,0:T(8,128)S(1)} %add.292), channel_id=1, source_target_pairs={{8,0},{16,24},{9,1},{17,25},{10,2},{18,26},{11,3},{19,27},{12,4},{... | collective-permute-start | bytes 2359304 | tf_op jit(solution)/shard_map/ppermute | solution.py:381
  701.3 100.7 %collective-permute-start.55 = (f32[384,1024]{1,0:T(8,128)S(1)}, f32[384,1024]{1,0:T(8,128)S(1)}, u32[]{:S(2)}, u32[]{:S(2)}) collective-permute-start(f32[384,1024]{1,0:T(8,128)S(1)} %add.285), channel_id=1, source_target_pairs={{8,0},{16,24},{9,1},{17,25},{10,2},{18,26},{11,3},{19,27},{12,4},{... | collective-permute-start | bytes 4718600 | tf_op jit(solution)/shard_map/ppermute | solution.py:381
  708.2 92.5 %collective-permute-start.30 = (f32[576,384]{1,0:T(8,128)S(1)}, f32[576,384]{1,0:T(8,128)S(1)}, u32[]{:S(2)}, u32[]{:S(2)}) collective-permute-start(f32[576,384]{1,0:T(8,128)S(1)} %add.250), channel_id=1, source_target_pairs={{8,0},{16,24},{9,1},{17,25},{10,2},{18,26},{11,3},{19,27},{12,4},{... | collective-permute-start | bytes 2654216 | tf_op jit(solution)/shard_map/ppermute | solution.py:381
  712.2 121.6 %collective-permute-start.50 = (f32[384,1024]{1,0:T(8,128)S(1)}, f32[384,1024]{1,0:T(8,128)}, u32[]{:S(2)}, u32[]{:S(2)}) collective-permute-start(f32[384,1024]{1,0:T(8,128)S(1)} %add.278), channel_id=1, source_target_pairs={{8,0},{16,24},{9,1},{17,25},{10,2},{18,26},{11,3},{19,27},{12,4},{... | collective-permute-start | bytes 4718600 | tf_op jit(solution)/shard_map/ppermute | solution.py:381
  (225 other events, 2704.9 us)
Sparse Core Ops, SparseCore 0:
  560.1 123.8 all-reduce.1
